TPU v7x, 256 devices: a whole 4x4x8 slice. The times are simulated.
256 devices in a mesh: view: 8 (over z), head: 32 (over y, x, core).
Axes of the slice: x: 4, y: 4, z: 8, core: 2. Of those that a mesh axis runs over, the one named last changes fastest.
Arguments:
- query_tokens: bfloat16 [32768, 4096], P(('view', 'head')), may hold values from -5 to 5
- key_tokens: bfloat16 [32768, 4096], P(('view', 'head')), may hold values from -5 to 5
- value_tokens: bfloat16 [32768, 4096], P(('view', 'head')), may hold values from -6 to 6
- cotangent: bfloat16 [32768, 4096], P(('view', 'head')), may hold values from -6 to 6
- neighbors: int32 [64, 2], replicated, may hold values from 0 to 63, as said below
- view_slot: int32 [64], replicated, may hold values from 0 to 63, as said below
Outputs:
- attended: bfloat16 [32768, 4096], P(('view', 'head'))
- query_grads: bfloat16 [32768, 4096], P(('view', 'head'))
- key_grads: bfloat16 [32768, 4096], P(('view', 'head'))
- value_grads: bfloat16 [32768, 4096], P(('view', 'head'))
Inputs may be any that keep to these rules, and one draw needn't show every extreme that they name: `view_slot`: A permutation of the views. `neighbors`: entry 0 of row v is v. Every other entry either repeats v or names a distinct view whose slot lies in another group than v's. The views that the views of one group name in any single other group are at most 1, and some group names exactly 1 in every other group; the views of one group named by views of other groups are exactly 2 for every group.
All inputs are finite; a program needn't handle non-finite values.
Results may differ from a plain program's by a relative error of at most 0.023.
Values may be sent and summed in bfloat16 or wider, within the bound.
A program may use at most 128 MiB of HBM per device.

v0:
```python
import math

import jax
import jax.numpy as jnp
from jax import lax
from jax.sharding import PartitionSpec as P

HD = 128
EXP = 2


def link_tables(neighbors, view_slot, groups):
    view_total = neighbors.shape[0]
    per_group = view_total // groups
    slot_range = jnp.arange(view_total, dtype=jnp.int32)
    owner_match = view_slot[None, :] == slot_range[:, None]
    view_of_slot = jnp.sum(jnp.where(owner_match, slot_range[None, :], 0), axis=1)
    slot_lists = view_slot[neighbors[view_of_slot]]
    linked = jnp.any(slot_lists[:, :, None] == slot_range[None, None, :], axis=1)
    slot_group = slot_range // per_group
    remote = linked & (slot_group[:, None] != slot_group[None, :])
    wanted = jnp.any(remote.reshape(groups, per_group, view_total), axis=1).reshape(
        groups, groups, per_group
    )
    exported = jnp.any(wanted, axis=0)
    return (slot_lists, wanted, exported)


def ranked(flag_table, slot_count):
    entries = flag_table.shape[-1]
    rank_table = jnp.cumsum(flag_table.astype(jnp.int32), axis=-1) - 1
    target_rank = jnp.arange(slot_count, dtype=jnp.int32)[:, None]
    matched = flag_table[..., None, :] & (rank_table[..., None, :] == target_rank)
    chosen = jnp.sum(jnp.where(matched, jnp.arange(entries, dtype=jnp.int32), 0), axis=-1)
    return (chosen, jnp.any(matched, axis=-1), rank_table)


def on_device(query_tokens, key_tokens, value_tokens, cotangent, neighbors, view_slot):
    groups = lax.axis_size("view")
    own_group = lax.axis_index("view")
    query_head, key_head, value_head, grad_head = (
        lax.all_to_all(query_tokens, "head", split_axis=1, concat_axis=0, tiled=True),
        lax.all_to_all(key_tokens, "head", split_axis=1, concat_axis=0, tiled=True),
        lax.all_to_all(value_tokens, "head", split_axis=1, concat_axis=0, tiled=True),
        lax.all_to_all(cotangent, "head", split_axis=1, concat_axis=0, tiled=True),
    )
    row_total, feature = query_head.shape
    view_total = neighbors.shape[0]
    per_group = view_total // groups
    length = row_total // per_group
    list_width = neighbors.shape[1]
    head_count = feature // HD
    score_scale = 1.0 / math.sqrt(HD)
    slot_lists, wanted, exported = link_tables(neighbors, view_slot, groups)
    local_pairs = jnp.concatenate([key_head, value_head], axis=1).reshape(
        per_group, length, 2 * feature
    )
    slot_range = jnp.arange(view_total, dtype=jnp.int32)
    slot_group = slot_range // per_group
    export_index, export_valid, export_rank = ranked(exported, EXP)
    own_export = lax.dynamic_index_in_dim(export_index, own_group, 0, keepdims=False)
    arrived = lax.all_gather(local_pairs[own_export], "view", axis=0, tiled=True)
    stride = EXP
    offset_table = export_rank.reshape(view_total)
    key_pool = jnp.concatenate([local_pairs, arrived], axis=0)
    pool_slot = jnp.where(
        slot_group == own_group,
        slot_range % per_group,
        per_group + slot_group * stride + offset_table,
    )
    own_lists = lax.dynamic_slice_in_dim(slot_lists, own_group * per_group, per_group, 0)
    own_pool = pool_slot[own_lists]

    def attend(position, loop_state):
        attended, query_grad, pair_grads = loop_state
        row_start = position * length
        query_block = lax.dynamic_slice_in_dim(query_head, row_start, length, 0).reshape(
            length, head_count, HD
        )
        grad_block = lax.dynamic_slice_in_dim(grad_head, row_start, length, 0).reshape(
            length, head_count, HD
        )
        pool_rows = own_pool[position]
        own_slot = own_group * per_group + position
        allowed = (jnp.arange(list_width, dtype=jnp.int32) == 0) | (own_lists[position] != own_slot)
        gathered = key_pool[pool_rows]
        key_block = gathered[:, :, :feature].reshape(list_width, length, head_count, HD)
        value_block = gathered[:, :, feature:].reshape(list_width, length, head_count, HD)
        scores = (
            jnp.einsum("qhd,nkhd->hqnk", query_block, key_block, preferred_element_type=jnp.float32)
            * score_scale
        )
        scores = jnp.where(allowed[None, None, :, None], scores, -jnp.inf)
        highest = jnp.max(scores, axis=(2, 3), keepdims=True)
        log_total = highest + jnp.log(
            jnp.sum(jnp.exp(scores - highest), axis=(2, 3), keepdims=True)
        )
        weights = jnp.exp(scores - log_total)
        weights_bf = weights.astype(jnp.bfloat16)
        out_block = jnp.einsum(
            "hqnk,nkhd->qhd", weights_bf, value_block, preferred_element_type=jnp.float32
        ).astype(jnp.bfloat16)
        row_delta = jnp.sum(grad_block.astype(jnp.float32) * out_block.astype(jnp.float32), axis=2)
        weight_grad = jnp.einsum(
            "qhd,nkhd->hqnk", grad_block, value_block, preferred_element_type=jnp.float32
        )
        dscore = (weights * (weight_grad - row_delta.T[:, :, None, None])).astype(jnp.bfloat16)
        query_part = (
            jnp.einsum("hqnk,nkhd->qhd", dscore, key_block, preferred_element_type=jnp.float32)
            * score_scale
        ).astype(jnp.bfloat16)
        key_part = (
            jnp.einsum("hqnk,qhd->nkhd", dscore, query_block, preferred_element_type=jnp.float32)
            * score_scale
        )
        value_part = jnp.einsum(
            "hqnk,qhd->nkhd", weights_bf, grad_block, preferred_element_type=jnp.float32
        )
        pair_part = jnp.concatenate(
            [
                key_part.reshape(list_width, length, feature),
                value_part.reshape(list_width, length, feature),
            ],
            axis=2,
        )
        pair_grads = pair_grads.at[pool_rows].add(pair_part)
        attended = lax.dynamic_update_slice_in_dim(
            attended, out_block.reshape(length, feature), row_start, 0
        )
        query_grad = lax.dynamic_update_slice_in_dim(
            query_grad, query_part.reshape(length, feature), row_start, 0
        )
        return (attended, query_grad, pair_grads)

    start_rows = jnp.zeros((row_total, feature), jnp.bfloat16)
    start_grads = jnp.zeros((key_pool.shape[0], length, 2 * feature), jnp.float32)
    attended, query_grad, pair_grads = lax.fori_loop(
        0, per_group, attend, (start_rows, start_rows, start_grads)
    )
    local_sum = lax.optimization_barrier(pair_grads[:per_group].astype(jnp.bfloat16)).astype(
        jnp.float32
    )
    returned = lax.psum_scatter(
        pair_grads[per_group:].astype(jnp.bfloat16), "view", scatter_dimension=0, tiled=True
    ).astype(jnp.float32)
    own_valid = lax.dynamic_index_in_dim(export_valid, own_group, 0, keepdims=False)
    owner_total = local_sum.at[own_export].add(jnp.where(own_valid[:, None, None], returned, 0.0))
    key_final = owner_total.astype(jnp.bfloat16)
    key_grad = key_final[:, :, :feature].reshape(row_total, feature)
    value_grad = key_final[:, :, feature:].reshape(row_total, feature)
    return (
        lax.all_to_all(attended, "head", split_axis=0, concat_axis=1, tiled=True),
        lax.all_to_all(query_grad, "head", split_axis=0, concat_axis=1, tiled=True),
        lax.all_to_all(key_grad, "head", split_axis=0, concat_axis=1, tiled=True),
        lax.all_to_all(value_grad, "head", split_axis=0, concat_axis=1, tiled=True),
    )


def solution(mesh):
    in_specs = (
        P(("view", "head"), None),
        P(("view", "head"), None),
        P(("view", "head"), None),
        P(("view", "head"), None),
        P(),
        P(),
    )
    out_specs = (
        P(("view", "head"), None),
        P(("view", "head"), None),
        P(("view", "head"), None),
        P(("view", "head"), None),
    )
    return jax.shard_map(
        on_device, mesh=mesh, in_specs=in_specs, out_specs=out_specs, check_vma=False
    )
```

profile of v0, /device:TPU:3, one launch (start us, length us, event | category | flops | bytes accessed | tf_op | source)
XLA Modules:
  0.0 367.5 jit_solution(13804364019875590391)
XLA Ops:
  9.7 7.9 %all-to-all-start = ((bf16[128,32,128]{2,0,1:T(8,128)(2,1)}), bf16[128,32,128]{2,0,1:T(8,128)(2,1)S(1)}, u32[]{:S(2)}, u32[]{:S(2)}) async-start(bf16[128,32,128]{2,0,1:T(8,128)(2,1)} %copy_bitcast_fusion.2), calls=%async_computation | async-start | bytes 2097152 | tf_op jit(solution)/shard_map/all_to_all | solution.py:43
  21.6 12.1 %all-to-all-done = bf16[128,32,128]{2,0,1:T(8,128)(2,1)S(1)} async-done(((bf16[128,32,128]{2,0,1:T(8,128)(2,1)}), bf16[128,32,128]{2,0,1:T(8,128)(2,1)S(1)}, u32[]{:S(2)}, u32[]{:S(2)}) %all-to-all-start) | async-done | bytes 1048608 | tf_op jit(solution)/shard_map/all_to_all | solution.py:43
  33.8 5.0 %all-to-all-start.1 = ((bf16[128,32,128]{2,0,1:T(8,128)(2,1)}), bf16[128,32,128]{2,0,1:T(8,128)(2,1)S(1)}, u32[]{:S(2)}, u32[]{:S(2)}) async-start(bf16[128,32,128]{2,0,1:T(8,128)(2,1)} %copy_bitcast_fusion.1), calls=%async_computation.1 | async-start | bytes 2097152 | tf_op jit(solution)/shard_map/all_to_all | solution.py:44
  39.8 15.3 %all-to-all-done.1 = bf16[128,32,128]{2,0,1:T(8,128)(2,1)S(1)} async-done(((bf16[128,32,128]{2,0,1:T(8,128)(2,1)}), bf16[128,32,128]{2,0,1:T(8,128)(2,1)S(1)}, u32[]{:S(2)}, u32[]{:S(2)}) %all-to-all-start.1) | async-done | bytes 1048608 | tf_op jit(solution)/shard_map/all_to_all | solution.py:44
  55.0 1.6 pad_maximum_fusion.2
  56.6 3.0 gather_fusion.4
  60.9 5.0 %all-to-all-start.3 = ((bf16[128,32,128]{0,2,1:T(8,128)(2,1)}), bf16[128,32,128]{0,2,1:T(8,128)(2,1)S(1)}, u32[]{:S(2)}, u32[]{:S(2)}) async-start(bf16[128,32,128]{0,2,1:T(8,128)(2,1)} %bitcast.161), calls=%async_computation.3 | async-start | bytes 2097152 | tf_op jit(solution)/shard_map/all_to_all | solution.py:45
  65.9 2.5 copy_bitcast_fusion
  68.4 13.8 %all-to-all-done.3 = bf16[128,32,128]{0,2,1:T(8,128)(2,1)S(1)} async-done(((bf16[128,32,128]{0,2,1:T(8,128)(2,1)}), bf16[128,32,128]{0,2,1:T(8,128)(2,1)S(1)}, u32[]{:S(2)}, u32[]{:S(2)}) %all-to-all-start.3) | async-done | bytes 1048608 | tf_op jit(solution)/shard_map/all_to_all | solution.py:45
  82.2 5.7 %all-to-all-start.2 = ((bf16[128,32,128]{2,0,1:T(8,128)(2,1)}), bf16[128,32,128]{2,0,1:T(8,128)(2,1)}, u32[]{:S(2)}, u32[]{:S(2)}) async-start(bf16[128,32,128]{2,0,1:T(8,128)(2,1)} %copy_bitcast_fusion), calls=%async_computation.2 | async-start | bytes 2097152 | tf_op jit(solution)/shard_map/all_to_all | solution.py:42
  88.9 2.3 copy.147
  91.1 23.2 %all-gather.3.cloned.1.call-done = bf16[16,512,256]{2,1,0:T(8,128)(2,1)} async-done(((bf16[2,512,256]{2,1,0:T(8,128)(2,1)}), bf16[16,512,256]{2,1,0:T(8,128)(2,1)}) %all-gather.3.cloned.1.call-update) | async-done | bytes 4194320 | tf_op jit(solution)/shard_map/all_gather | solution.py:62
  114.3 5.8 %pad_maximum_fusion.1 = bf16[24,512,256]{2,1,0:T(8,128)(2,1)} fusion(bf16[16,512,256]{2,1,0:T(8,128)(2,1)} %all-gather.3.cloned.1.call-done, bf16[8,512,128]{2,1,0:T(8,128)(2,1)S(1)} %bitcast.159, bf16[8,512,128]{2,1,0:T(8,128)(2,1)S(1)} %bitcast.157), kind=kLoop, calls=%fused_computation.47 | loop fusion | flops 18874368 | bytes 12582912 | tf_op jit(solution)/shard_map/concatenate | solution.py:65
  122.4 6.0 %broadcast_in_dim.91 = f32[24,512,256]{2,1,0:T(8,128)} broadcast(f32[]{:T(128)} %constant.151.clone.1), dimensions={} | broadcast | bytes 12582916 | tf_op jit(solution)/shard_map/broadcast_in_dim | solution.py:136
  128.3 111.0 %while.19 = (s32[]{:T(128)}, bf16[4096,128]{1,0:T(8,128)(2,1)}, bf16[4096,128]{1,0:T(8,128)(2,1)}, f32[24,512,256]{2,1,0:T(8,128)}, s32[8,2]{1,0:T(8,128)S(1)}, ...) while((s32[]{:T(128)}, bf16[4096,128]{1,0:T(8,128)(2,1)}, ...), condition=%wide.region_10.11_spmd, body=%wide.region_5.10_spmd.sunk | while | flops 813236224 | bytes 26635028 | solution.py:137
  129.4 3.4 gather_fusion
  139.2 3.1 scatter_fusion
  143.3 3.4 gather_fusion
  153.1 3.1 scatter_fusion
  157.2 3.4 gather_fusion
  167.0 3.1 scatter_fusion
  171.1 3.4 gather_fusion
  180.9 3.1 scatter_fusion
  185.0 3.4 gather_fusion
  192.1 1.4 fusion.62
  194.8 2.9 scatter_fusion
  198.7 3.4 gather_fusion
  208.5 3.1 scatter_fusion
  212.6 3.4 gather_fusion
  222.4 3.1 scatter_fusion
  226.5 3.4 gather_fusion
  236.3 3.1 scatter_fusion
  239.4 8.0 %convert.5 = bf16[24,512,256]{2,1,0:T(8,128)(2,1)} convert(f32[24,512,256]{2,1,0:T(8,128)} %get-tuple-element.241) | non-fusion elementwise | flops 3145728 | bytes 18874368 | tf_op jit(solution)/shard_map/convert.2
  247.4 4.5 %slice.49 = bf16[16,512,256]{2,1,0:T(8,128)(2,1)} slice(bf16[24,512,256]{2,1,0:T(8,128)(2,1)} %convert.5), slice={[8:24], [0:512], [0:256]} | slice | bytes 8388608 | tf_op jit(solution)/shard_map/slice | solution.py:144
  253.2 23.7 %all_to_all.146 = bf16[32,128,128]{2,1,0:T(8,128)(2,1)S(1)} all-to-all(bf16[32,128,128]{2,1,0:T(8,128)(2,1)S(1)} %bitcast.160), channel_id=1, replica_groups=mesh['view'=8,'head'=32] {'head'}, dimensions={0} | all-to-all | bytes 2097152 | tf_op jit(solution)/shard_map/all_to_all | solution.py:152
  276.8 5.2 %all-to-all-start.5 = ((bf16[32,128,128]{2,1,0:T(8,128)(2,1)}), bf16[32,128,128]{2,1,0:T(8,128)(2,1)S(1)}, u32[]{:S(2)}, u32[]{:S(2)}) async-start(bf16[32,128,128]{2,1,0:T(8,128)(2,1)} %bitcast.39), calls=%async_computation.5 | async-start | bytes 2097152 | tf_op jit(solution)/shard_map/all_to_all | solution.py:153
  282.4 1.6 slice-done
  284.0 2.3 convert_element_type.86
  286.3 19.2 %reduce-scatter.2.cloned.1.call-done = bf16[2,512,256]{2,1,0:T(8,128)(2,1)} async-done(((bf16[16,512,256]{2,1,0:T(8,128)(2,1)}), bf16[2,512,256]{2,1,0:T(8,128)(2,1)}) %reduce-scatter.2.cloned.1.call-update) | async-done | bytes 524304 | tf_op jit(solution)/shard_map/reduce_scatter | solution.py:143
  306.7 3.1 scatter_fusion.1
  309.8 2.4 convert_element_type.88
  312.2 1.5 fusion.31
  313.7 23.7 %all_to_all.147 = bf16[32,128,128]{2,1,0:T(8,128)(2,1)} all-to-all(bf16[32,128,128]{2,1,0:T(8,128)(2,1)S(1)} %bitcast.167), channel_id=1, replica_groups=mesh['view'=8,'head'=32] {'head'}, dimensions={0} | all-to-all | bytes 2097152 | tf_op jit(solution)/shard_map/all_to_all | solution.py:154
  337.4 5.0 %all-to-all-start.7 = ((bf16[32,128,128]{2,1,0:T(8,128)(2,1)}), bf16[32,128,128]{2,1,0:T(8,128)(2,1)S(1)}, u32[]{:S(2)}, u32[]{:S(2)}) async-start(bf16[32,128,128]{2,1,0:T(8,128)(2,1)} %bitcast.166), calls=%async_computation.8 | async-start | bytes 2097152 | tf_op jit(solution)/shard_map/all_to_all | solution.py:155
  343.8 2.3 copy.155
  347.3 2.3 copy.156
  350.9 2.4 copy.157
  353.2 5.5 %all-to-all-done.7 = bf16[32,128,128]{2,1,0:T(8,128)(2,1)S(1)} async-done(((bf16[32,128,128]{2,1,0:T(8,128)(2,1)}), bf16[32,128,128]{2,1,0:T(8,128)(2,1)S(1)}, u32[]{:S(2)}, u32[]{:S(2)}) %all-to-all-start.7) | async-done | bytes 1048608 | tf_op jit(solution)/shard_map/all_to_all | solution.py:155
  (216 shorter events, 78.1 us)
Async XLA Ops:
  7.2 1.2 copy-start
  7.2 10.4 %copy-start.2 = (s32[64]{0:T(128)S(1)}, s32[64]{0:T(128)}, u32[]{:S(2)}) copy-start(s32[64]{0:T(128)} %param.13) | copy-start | bytes 772
  7.2 10.5 %copy-start.8 = (s32[64,2]{0,1:T(2,128)S(1)}, s32[64,2]{0,1:T(2,128)}, u32[]{:S(2)}) copy-start(s32[64,2]{0,1:T(2,128)} %param.12) | copy-start | bytes 1540
  9.7 24.1 %all-to-all-start = ((bf16[128,32,128]{2,0,1:T(8,128)(2,1)}), bf16[128,32,128]{2,0,1:T(8,128)(2,1)S(1)}, u32[]{:S(2)}, u32[]{:S(2)}) async-start(bf16[128,32,128]{2,0,1:T(8,128)(2,1)} %copy_bitcast_fusion.2), calls=%async_computation | async-start | bytes 2097152 | tf_op jit(solution)/shard_map/all_to_all | solution.py:43
  18.8 1.6 copy-start.6
  33.8 21.3 %all-to-all-start.1 = ((bf16[128,32,128]{2,0,1:T(8,128)(2,1)}), bf16[128,32,128]{2,0,1:T(8,128)(2,1)S(1)}, u32[]{:S(2)}, u32[]{:S(2)}) async-start(bf16[128,32,128]{2,0,1:T(8,128)(2,1)} %copy_bitcast_fusion.1), calls=%async_computation.1 | async-start | bytes 2097152 | tf_op jit(solution)/shard_map/all_to_all | solution.py:44
  38.8 75.5 %all-gather.3.cloned.1.call-start = ((), (), s32[]{:S(2)}) async-start(), calls=%async_computation.10 | async-start | bytes 4718592 | tf_op jit(solution)/shard_map/all_gather | solution.py:62
  55.0 4.6 %copy-start.7 = (bf16[128,4096]{1,0:T(8,128)(2,1)S(1)}, bf16[128,4096]{1,0:T(8,128)(2,1)}, u32[]{:S(2)}) copy-start(bf16[128,4096]{1,0:T(8,128)(2,1)} %param.11) | copy-start | bytes 3145732
  60.9 21.3 %all-to-all-start.3 = ((bf16[128,32,128]{0,2,1:T(8,128)(2,1)}), bf16[128,32,128]{0,2,1:T(8,128)(2,1)S(1)}, u32[]{:S(2)}, u32[]{:S(2)}) async-start(bf16[128,32,128]{0,2,1:T(8,128)(2,1)} %bitcast.161), calls=%async_computation.3 | async-start | bytes 2097152 | tf_op jit(solution)/shard_map/all_to_all | solution.py:45
  82.2 5.9 %copy-start.3 = (bf16[128,32,128]{0,2,1:T(8,128)(2,1)}, bf16[128,32,128]{0,2,1:T(8,128)(2,1)S(1)}, u32[]{:S(2)}) copy-start(bf16[128,32,128]{0,2,1:T(8,128)(2,1)S(1)} %all-to-all-done.3) | copy-start | bytes 3145732
  82.2 37.9 %all-to-all-start.2 = ((bf16[128,32,128]{2,0,1:T(8,128)(2,1)}), bf16[128,32,128]{2,0,1:T(8,128)(2,1)}, u32[]{:S(2)}, u32[]{:S(2)}) async-start(bf16[128,32,128]{2,0,1:T(8,128)(2,1)} %copy_bitcast_fusion), calls=%async_computation.2 | async-start | bytes 2097152 | tf_op jit(solution)/shard_map/all_to_all | solution.py:42
  87.9 217.7 %reduce-scatter.2.cloned.1.call-start = ((), (), s32[]{:S(2)}) async-start(), calls=%async_computation.9 | async-start | bytes 4718592 | tf_op jit(solution)/shard_map/reduce_scatter | solution.py:143
  251.9 1.2 copy-start.5
  276.8 36.9 %all-to-all-start.5 = ((bf16[32,128,128]{2,1,0:T(8,128)(2,1)}), bf16[32,128,128]{2,1,0:T(8,128)(2,1)S(1)}, u32[]{:S(2)}, u32[]{:S(2)}) async-start(bf16[32,128,128]{2,1,0:T(8,128)(2,1)} %bitcast.39), calls=%async_computation.5 | async-start | bytes 2097152 | tf_op jit(solution)/shard_map/all_to_all | solution.py:153
  282.4 1.6 slice-start
  337.4 21.3 %all-to-all-start.7 = ((bf16[32,128,128]{2,1,0:T(8,128)(2,1)}), bf16[32,128,128]{2,1,0:T(8,128)(2,1)S(1)}, u32[]{:S(2)}, u32[]{:S(2)}) async-start(bf16[32,128,128]{2,1,0:T(8,128)(2,1)} %bitcast.166), calls=%async_computation.8 | async-start | bytes 2097152 | tf_op jit(solution)/shard_map/all_to_all | solution.py:155
  346.0 3.6 copy-start.4
  350.9 9.8 %copy-start.1 = (bf16[128,4096]{1,0:T(8,128)(2,1)S(1)}, bf16[128,4096]{1,0:T(8,128)(2,1)}, u32[]{:S(2)}) copy-start(bf16[128,4096]{1,0:T(8,128)(2,1)} %param.9) | copy-start | bytes 3145732
Sparse Core Ops, SparseCore 0:
  59.7 54.5 all-gather.2
  252.1 53.4 reduce-scatter.1
where the time goes:
time: 371 us; the launch traced here: 368 us
  local copies, waits for them, and re-layouts  92.1 us (25%)
  waiting for transfers between devices  89.1 us (24%)
  other arithmetic  53.3 us (14%)
  blocking collectives  47.4 us (13%)
  matrix products  36.7 us (10%)
  starting transfers between devices  33.9 us (9%)
  between operations  14.3 us (4%)
    gather x8, local copies, waits for them, and re-layouts, attend(): gathered = key_pool[pool_rows]  26.9 us
    scatter-add x8, other arithmetic, attend(): pair_grads = pair_grads.at[pool_rows].add(pair_part)  24.3 us
    all_to_all x1, blocking collectives, on_device(): lax.all_to_all(key_grad, 'head', split_axis=0, concat_axis=1, tiled=True)  23.7 us
    all_to_all x1, blocking collectives, on_device(): lax.all_to_all(attended, 'head', split_axis=0, concat_axis=1, tiled=True)  23.7 us
    all_gather x1, waiting for transfers between devices, on_device(): lax.all_gather(local_pairs[own_export], 'view', axis=0, tiled=True)  23.2 us
    reduce_scatter x1, waiting for transfers between devices, on_device(): lax.psum_scatter(pair_grads[per_group:].astype(jnp.bfloat16), 'view', sca...  19.2 us
    all_to_all x1, waiting for transfers between devices, on_device(): lax.all_to_all(value_tokens, 'head', split_axis=1, concat_axis=0, tiled=T...  15.3 us
    all_to_all x1, waiting for transfers between devices, on_device(): lax.all_to_all(cotangent, 'head', split_axis=1, concat_axis=0, tiled=True)  13.8 us
  transfers between devices with their start and end apart: 8, of which 6 were waited for; matrix products, arithmetic and copies ran while one was open for 11% of the time, Pallas kernels for 0%

commit v1 on v0

v1 whole, which is shorter than its diff:
```python
import functools
import math

import jax
import jax.numpy as jnp
from jax import lax
from jax.experimental import pallas as pl
from jax.experimental.pallas import tpu as pltpu
from jax.sharding import PartitionSpec as P

MESH = pl.DeviceIdType.MESH
GROUPS = 8
HEADS = 32
PER_GROUP = 8
RANKS = 4
ROWS = 128
HD = 128
LENGTH = 512
OTHERS = GROUPS - 1
SCALE = 1.0 / math.sqrt(HD)
EXP2_SCALE = math.log2(math.e) / math.sqrt(HD)
BF = jnp.bfloat16
F32 = jnp.float32


def dot_nt(a, b):
    return lax.dot_general(a, b, (((1,), (1,)), ((), ())), preferred_element_type=F32)


def dot_nn(a, b):
    return lax.dot_general(a, b, (((1,), (0,)), ((), ())), preferred_element_type=F32)


def kernel(
    neighbors, view_slot, q_in, k_in, v_in, g_in,
    o_out, dq_out, dk_out, dv_out,
    qh, kh, vh, gh,
    send_k, send_v, far_k, far_v,
    oh, dqh, dkh, dvh,
    acc_k, acc_v, ret_k, ret_v, back_k, back_v,
    table,
    in_send, in_recv, z_send, z_recv, ret_send, ret_recv_k, ret_recv_v, out_send, out_recv,
):
    group = lax.axis_index("view")
    head = lax.axis_index("head")
    row_y, col_x, core = head // 8, (head // 2) % 4, head % 2

    def plane_peer(step):
        dy, dx, dc = step // 8, (step // 2) % 4, step % 2
        return (((row_y + dy) % 4) * 4 + (col_x + dx) % 4) * 2 + (core + dc) % 2

    def for_peers(body):
        def run(step, carry):
            body(plane_peer(step))
            return carry

        lax.fori_loop(1, HEADS, run, 0)

    def columns(index):
        return pl.ds(pl.multiple_of(index * HD, HD), HD)

    barrier = pltpu.get_barrier_semaphore()

    def greet(peer):
        pl.semaphore_signal(barrier, inc=1, device_id=(group, peer), device_id_type=MESH)

    for_peers(greet)
    for step in range(1, GROUPS):
        pl.semaphore_signal(
            barrier, inc=1, device_id=((group + step) % GROUPS, head), device_id_type=MESH
        )
    pl.semaphore_wait(barrier, HEADS - 1 + OTHERS)

    def scatter_heads(index, source, target):
        def send(peer):
            pltpu.make_async_remote_copy(
                src_ref=source.at[:, columns(peer)],
                dst_ref=target.at[head],
                send_sem=in_send.at[index],
                recv_sem=in_recv.at[index],
                device_id=(group, peer),
                device_id_type=MESH,
            ).start()

        for_peers(send)
        pltpu.make_async_copy(
            source.at[:, columns(head)], target.at[head], in_recv.at[index]
        ).start()

    def wait_heads(index, target):
        pltpu.make_async_copy(target, target, in_recv.at[index]).wait()

    scatter_heads(0, k_in, kh)
    scatter_heads(1, v_in, vh)

    def read_links(view, carry):
        slots, wanted = carry
        slot = view_slot[view]
        other = view_slot[neighbors[view, 1]]
        slot_group, slot_place = slot >> 3, slot & 7
        other_group, other_place = other >> 3, other & 7
        source = (other_group - group + 7) & 7
        reader = (slot_group - group + 7) & 7
        own = slot_group == group
        read = (other_group == group) & (reader != 7)
        slots = tuple(
            jnp.where(own & (slot_place == place), source, slots[place])
            for place in range(PER_GROUP)
        )
        wanted = tuple(
            jnp.where(read & (reader == index), other_place, wanted[index])
            for index in range(OTHERS)
        )
        return slots, wanted

    slots, wanted = lax.fori_loop(
        0,
        PER_GROUP * GROUPS,
        read_links,
        ((jnp.int32(7),) * PER_GROUP, (jnp.int32(-1),) * OTHERS),
    )
    for place in range(PER_GROUP):
        table[0, place] = jnp.where(slots[place] == 7, 0, slots[place])
        table[1, place] = jnp.where(slots[place] == 7, 1, 0)
        before = jnp.int32(-1)
        for earlier in range(place):
            before = jnp.where(
                (slots[earlier] == slots[place]) & (slots[place] != 7), earlier, before
            )
        table[2, place] = before

    def exchange(index, source, stage, target):
        for reader in (3, 2, 4, 1, 5, 0, 6):
            place = jnp.maximum(wanted[reader], 0)
            stage[reader] = source[pl.ds(place * RANKS, RANKS)]
            pltpu.make_async_remote_copy(
                src_ref=stage.at[reader],
                dst_ref=target.at[OTHERS - 1 - reader],
                send_sem=z_send.at[index],
                recv_sem=z_recv.at[index],
                device_id=((group + 1 + reader) % GROUPS, head),
                device_id_type=MESH,
            ).start()

    wait_heads(0, kh)
    exchange(0, kh, send_k, far_k)
    scatter_heads(2, q_in, qh)
    wait_heads(1, vh)
    exchange(1, vh, send_v, far_v)
    scatter_heads(3, g_in, gh)
    wait_heads(2, qh)
    wait_heads(3, gh)
    for index, target in ((0, far_k), (1, far_v)):
        pltpu.make_async_copy(target, target, z_recv.at[index]).wait()

    def attend(place, carry):
        source = table[0, place]
        off = table[1, place].astype(F32) * 1e30
        before = table[2, place]
        rows = pl.ds(place * RANKS, RANKS)
        k, v = kh[rows].reshape(LENGTH, HD), vh[rows].reshape(LENGTH, HD)
        q, g = qh[rows].reshape(LENGTH, HD), gh[rows].reshape(LENGTH, HD)
        rk, rv = far_k[source].reshape(LENGTH, HD), far_v[source].reshape(LENGTH, HD)
        s_own, s_far = dot_nt(k, q), dot_nt(rk, q)
        highest = EXP2_SCALE * jnp.maximum(
            jnp.max(s_own, 0, keepdims=True), jnp.max(s_far, 0, keepdims=True) - off
        )
        e_own = jnp.exp2(s_own * EXP2_SCALE - highest)
        e_far = jnp.exp2(s_far * EXP2_SCALE - (highest + off))
        inverse = 1.0 / (jnp.sum(e_own, 0, keepdims=True) + jnp.sum(e_far, 0, keepdims=True))
        w_own, w_far = e_own * inverse, e_far * inverse
        b_own, b_far = w_own.astype(BF), w_far.astype(BF)
        out = (dot_nn(v.T, b_own) + dot_nn(rv.T, b_far)).astype(BF)
        oh[rows] = out.T.reshape(RANKS, ROWS, HD)
        delta = jnp.sum(g.T.astype(F32) * out.astype(F32), 0, keepdims=True)
        d_own = (w_own * (dot_nt(v, g) - delta)).astype(BF)
        d_far = (w_far * (dot_nt(rv, g) - delta)).astype(BF)
        grad = ((dot_nn(k.T, d_own) + dot_nn(rk.T, d_far)) * SCALE).astype(BF)
        dqh[rows] = grad.T.reshape(RANKS, ROWS, HD)
        dkh[rows] = (dot_nn(d_own, q) * SCALE).astype(BF).reshape(RANKS, ROWS, HD)
        dvh[rows] = dot_nn(b_own, g).astype(BF).reshape(RANKS, ROWS, HD)
        chained = jnp.maximum(before, 0)
        old_k, old_v = acc_k[chained], acc_v[chained]
        acc_k[place] = dot_nn(d_far, q) * SCALE + jnp.where(before >= 0, old_k, 0.0)
        acc_v[place] = dot_nn(b_far, g) + jnp.where(before >= 0, old_v, 0.0)
        return carry

    lax.fori_loop(0, PER_GROUP, attend, 0)

    returns = ((acc_k, ret_k, back_k, ret_recv_k), (acc_v, ret_v, back_v, ret_recv_v))
    last = []
    for source in range(OTHERS):
        final = jnp.int32(0)
        for place in range(PER_GROUP):
            final = jnp.where(slots[place] == source, place, final)
        last.append(final)
    for index, (acc, ret, back, recv) in enumerate(returns):
        for source in (3, 2, 4, 1, 5, 0, 6):
            ret[source] = acc[last[source]].astype(BF).reshape(RANKS, ROWS, HD)
    for rank in range(RANKS):
        for index, (acc, ret, back, recv) in enumerate(returns):
            for source in (3, 2, 4, 1, 5, 0, 6):
                pltpu.make_async_remote_copy(
                    src_ref=ret.at[source, rank],
                    dst_ref=back.at[rank, OTHERS - 1 - source],
                    send_sem=ret_send.at[index],
                    recv_sem=recv.at[rank],
                    device_id=((group + 1 + source) % GROUPS, head),
                    device_id_type=MESH,
                ).start()

    def gather_block(index, block, source, target):
        pltpu.make_async_remote_copy(
            src_ref=source.at[block],
            dst_ref=target.at[:, columns(head)],
            send_sem=out_send.at[index],
            recv_sem=out_recv.at[index],
            device_id=(group, block),
            device_id_type=MESH,
        ).start()

    def gather_own(index, source, target):
        pltpu.make_async_copy(
            source.at[head], target.at[:, columns(head)], out_recv.at[index]
        ).start()

    for_peers(lambda peer: gather_block(0, peer, oh, o_out))
    gather_own(0, oh, o_out)
    for_peers(lambda peer: gather_block(1, peer, dqh, dq_out))
    gather_own(1, dqh, dq_out)

    first, second = jnp.int32(8), jnp.int32(-1)
    for reader in range(OTHERS):
        first = jnp.where(
            (wanted[reader] >= 0) & (wanted[reader] < first), wanted[reader], first
        )
        second = jnp.maximum(second, wanted[reader])

    for rank in range(RANKS):
        for index, (acc, ret, back, recv) in enumerate(returns):
            target = (dkh, dvh)[index]
            output = (dk_out, dv_out)[index]
            pltpu.make_async_copy(back.at[rank], back.at[rank], recv.at[rank]).wait()
            first_sum = jnp.zeros((ROWS, HD), F32)
            second_sum = jnp.zeros((ROWS, HD), F32)
            for reader in range(OTHERS):
                part = back[rank, reader].astype(F32)
                first_sum += jnp.where(wanted[reader] == first, part, 0.0)
                second_sum += jnp.where(wanted[reader] == second, part, 0.0)
            for place in range(PER_GROUP):
                block = place * RANKS + rank
                extra = jnp.where(
                    place == first, first_sum, jnp.where(place == second, second_sum, 0.0)
                )
                target[block] = (target[block].astype(F32) + extra).astype(BF)

                @pl.when(block != head)
                def _():
                    gather_block(2 + index, block, target, output)

                @pl.when(block == head)
                def _():
                    gather_own(2 + index, target, output)

    for index, output in enumerate((o_out, dq_out, dk_out, dv_out)):
        pltpu.make_async_copy(output, output, out_recv.at[index]).wait()
    for index, source in enumerate((kh, vh, qh, gh)):
        blocks = source.at[pl.ds(0, HEADS - 1)]
        pltpu.make_async_copy(blocks, blocks, in_send.at[index]).wait()
        pltpu.make_async_copy(blocks, blocks, out_send.at[index]).wait()
    for index, stage in ((0, send_k), (1, send_v)):
        pltpu.make_async_copy(stage, stage, z_send.at[index]).wait()
    for index, stage in ((0, ret_k), (1, ret_v)):
        pltpu.make_async_copy(stage, stage, ret_send.at[index]).wait()


def on_device(query_tokens, key_tokens, value_tokens, cotangent, neighbors, view_slot):
    heads_buffer = pltpu.VMEM((HEADS, ROWS, HD), BF)
    far_buffer = pltpu.VMEM((OTHERS, RANKS, ROWS, HD), BF)
    back_buffer = pltpu.VMEM((RANKS, OTHERS, ROWS, HD), BF)
    sum_buffer = pltpu.VMEM((PER_GROUP, LENGTH, HD), F32)
    dma = pltpu.SemaphoreType.DMA
    smem = pl.BlockSpec(memory_space=pltpu.SMEM)
    anywhere = pl.BlockSpec(memory_space=pl.ANY)
    out = jax.ShapeDtypeStruct(query_tokens.shape, BF)
    return pl.pallas_call(
        kernel,
        out_shape=(out,) * 4,
        in_specs=[smem] * 2 + [anywhere] * 4,
        out_specs=(anywhere,) * 4,
        scratch_shapes=[heads_buffer] * 4
        + [far_buffer] * 4
        + [heads_buffer] * 4
        + [sum_buffer] * 2
        + [far_buffer] * 2
        + [back_buffer] * 2
        + [pltpu.SMEM((3, PER_GROUP), jnp.int32)]
        + [dma((4,))] * 2
        + [dma((2,))] * 3
        + [dma((RANKS,))] * 2
        + [dma((4,))] * 2,
        compiler_params=pltpu.CompilerParams(
            collective_id=0, has_side_effects=True, vmem_limit_bytes=56 << 20
        ),
    )(neighbors, view_slot, query_tokens, key_tokens, value_tokens, cotangent)


def solution(mesh):
    rows = P(("view", "head"), None)
    return jax.shard_map(
        on_device,
        mesh=mesh,
        in_specs=(rows, rows, rows, rows, P(), P()),
        out_specs=(rows, rows, rows, rows),
        check_vma=False,
    )
```

time: 371 us -> 161 us (0.43)
  Pallas kernels: 0 us -> 153 us
  waiting for transfers between devices: 89.1 us -> 0 us
  local copies, waits for them, and re-layouts: 92.1 us -> 7.94 us
  other arithmetic: 53.3 us -> 0 us
  blocking collectives: 47.4 us -> 0 us
  matrix products: 36.7 us -> 0 us
  starting transfers between devices: 33.9 us -> 0 us
  between operations: 14.3 us -> 0.65 us
    pallas_call x0 -> x1, Pallas kernels: none -> 153 us  [on_device(): pl.pallas_call(kernel, out_shape=(out,) * 4, in_specs=[smem] * 2 + [anywh...]
    all_to_all x2 -> x0, blocking collectives: 47.4 us -> none  [the longest x1 23.7 us: on_device(): lax.all_to_all(key_grad, 'head', split_axis=0, concat_axis=1, tiled=True)]
    all_to_all x6 -> x0, waiting for transfers between devices: 46.6 us -> none  [the longest x1 15.3 us: on_device(): lax.all_to_all(value_tokens, 'head', split_axis=1, concat_axis=0, tiled=T...]
    dot_general x48 -> x0, matrix products: 36.7 us -> none  [the longest x8 11.1 us: attend(): jnp.einsum('hqnk,qhd->nkhd', dscore, query_block, preferred_element_type=...]
    all_to_all x6 -> x0, starting transfers between devices: 33.8 us -> none  [the longest x1 7.93 us: on_device(): lax.all_to_all(key_tokens, 'head', split_axis=1, concat_axis=0, tiled=True)]
    gather x16 -> x0, local copies, waits for them, and re-layouts: 32.7 us -> none  [the longest x8 26.9 us: attend(): gathered = key_pool[pool_rows]]
    scatter-add x9 -> x0, other arithmetic: 27.4 us -> none  [the longest x8 24.3 us: attend(): pair_grads = pair_grads.at[pool_rows].add(pair_part)]
    all_gather x1 -> x0, waiting for transfers between devices: 23.2 us -> none  [on_device(): lax.all_gather(local_pairs[own_export], 'view', axis=0, tiled=True)]
  transfers between devices with their start and end apart: 8 -> 0, of which waited for: 6 -> 0; matrix products, arithmetic and copies ran while one was open for 11% -> 0% of each run, Pallas kernels for 0% -> 0%
where the time goes in v1:
time: 161 us
  Pallas kernels  153 us (95%)
  local copies, waits for them, and re-layouts  7.94 us (5%)
    pallas_call x1, Pallas kernels, on_device(): pl.pallas_call(kernel, out_shape=(out,) * 4, in_specs=[smem] * 2 + [anywh...  153 us
    unnamed x11, local copies, waits for them, and re-layouts  7.94 us

profile of v1, /device:TPU:3, one launch (start us, length us, event | category | flops | bytes accessed | tf_op | source)
XLA Modules:
  0.0 161.1 jit_solution(14956153916523585601)
XLA Ops:
  0.6 1.4 copy.10.neighbors
  2.0 152.5 %shard_map.93 = (bf16[128,4096]{1,0:T(8,128)(2,1)}, bf16[128,4096]{1,0:T(8,128)(2,1)}, bf16[128,4096]{1,0:T(8,128)(2,1)}, bf16[128,4096]{1,0:T(8,128)(2,1)}) custom-call(s32[64,2]{1,0:T(8,128)} %copy.10.neighbors, s32[64]{0:T(128)} %view_slot.1, bf16[128,4096]{1,0:T(8,128)(2,1)} %q_in.1, bf16[128,4096]{1,0:T(8,128)(2,1)} %k_in.1, bf16[128,4096]{1,0:T(8,128)(2,1)} %v_in.1, ...), custom_call_target="tpu_custom_call" | custom-call | tf_op jit(solution)/shard_map/pallas_call | solution.py:286
  154.6 0.0 copy-start.2
  154.6 2.4 %copy.15 = bf16[128,4096]{1,0:T(8,128)(2,1)} copy(bf16[128,4096]{1,0:T(8,128)(2,1)} %get-tuple-element.8) | data formatting | bytes 2097152
  157.0 0.0 copy-done.2
  157.0 0.0 copy-start.1
  157.0 1.0 copy.16
  157.9 0.6 copy-done.1
  158.6 0.0 copy-start
  158.6 1.0 copy.17
  159.5 0.6 copy-done
  160.2 1.0 copy.18
Async XLA Ops:
  154.6 2.4 %copy-start.2 = (bf16[128,4096]{1,0:T(8,128)(2,1)S(1)}, bf16[128,4096]{1,0:T(8,128)(2,1)}, u32[]{:S(2)}) copy-start(bf16[128,4096]{1,0:T(8,128)(2,1)} %get-tuple-element.9) | copy-start | bytes 3145732
  157.0 1.6 copy-start.1
  158.6 1.6 copy-start

commit v2 on v1

v2 whole, which is shorter than its diff:
```python
import functools
import math

import jax
import jax.numpy as jnp
from jax import lax
from jax.experimental import pallas as pl
from jax.experimental.pallas import tpu as pltpu
from jax.sharding import PartitionSpec as P

MESH = pl.DeviceIdType.MESH
GROUPS = 8
HEADS = 32
PER_GROUP = 8
RANKS = 4
ROWS = 128
HD = 128
LENGTH = 512
OTHERS = GROUPS - 1
SCALE = 1.0 / math.sqrt(HD)
EXP2_SCALE = math.log2(math.e) / math.sqrt(HD)
BF = jnp.bfloat16
F32 = jnp.float32


def ring_distance(step):
    return min(step, 4 - step)


PEERS = sorted(
    (
        (dy, dx, dc)
        for dy in range(4)
        for dx in range(4)
        for dc in range(2)
        if (dy, dx, dc) != (0, 0, 0)
    ),
    key=lambda step: (-ring_distance(step[0]) - ring_distance(step[1]), step),
)

POOL_K = {7: (0, 2), 6: (2, 2), 5: (4, 2), 4: (6, 1), 1: (7, 2), 2: (9, 2), 3: (11, 1)}
POOL_V = {7: (0, 2), 6: (2, 2), 5: (4, 1), 1: (5, 2), 2: (7, 2), 3: (9, 2), 4: (11, 1)}
POOL = 12
CHOICES = ((5, 1), (2, 7), (6, 1), (3, 7))


def dot_nt(a, b):
    return lax.dot_general(a, b, (((1,), (1,)), ((), ())), preferred_element_type=F32)


def dot_nn(a, b):
    return lax.dot_general(a, b, (((1,), (0,)), ((), ())), preferred_element_type=F32)


def kernel(
    neighbors, view_slot, q_in, k_in, v_in, g_in,
    o_out, dq_out, dk_out, dv_out,
    qh, kh, vh, gh,
    stage_k, stage_v, chosen, pool_k, pool_v,
    oh, dqh, dkh, dvh,
    exp_own, out_own, stats, d_far_all,
    acc_k, acc_v, ret_k, ret_v, back_k, back_v,
    table,
    in_send, in_recv, z_send, z_recv_k, z_recv_v,
    ret_send, ret_recv_k, ret_recv_v, out_send, out_recv,
):
    group = lax.axis_index("view")
    head = lax.axis_index("head")
    row_y, col_x, core = head // 8, (head // 2) % 4, head % 2

    def for_peers(body):
        for dy, dx, dc in PEERS:
            body((((row_y + dy) % 4) * 4 + (col_x + dx) % 4) * 2 + (core + dc) % 2)

    def columns(index):
        return pl.ds(pl.multiple_of(index * HD, HD), HD)

    barrier = pltpu.get_barrier_semaphore()

    def greet(peer):
        pl.semaphore_signal(barrier, inc=1, device_id=(group, peer), device_id_type=MESH)

    for_peers(greet)
    for step in range(1, GROUPS):
        pl.semaphore_signal(
            barrier, inc=1, device_id=((group + step) % GROUPS, head), device_id_type=MESH
        )
    pl.semaphore_wait(barrier, HEADS - 1 + OTHERS)

    def scatter_heads(index, source, target):
        def send(peer):
            pltpu.make_async_remote_copy(
                src_ref=source.at[:, columns(peer)],
                dst_ref=target.at[head],
                send_sem=in_send.at[index],
                recv_sem=in_recv.at[index],
                device_id=(group, peer),
                device_id_type=MESH,
            ).start()

        for_peers(send)
        pltpu.make_async_copy(
            source.at[:, columns(head)], target.at[head], in_recv.at[index]
        ).start()

    def wait_heads(index, target):
        pltpu.make_async_copy(target, target, in_recv.at[index]).wait()

    scatter_heads(0, k_in, kh)
    scatter_heads(1, v_in, vh)

    def read_links(view, carry):
        named, lowest, highest, chosen_place, wanted = carry
        slot = view_slot[view]
        other = view_slot[neighbors[1, view]]
        slot_group, slot_place = slot >> 3, slot & 7
        other_group, other_place = other >> 3, other & 7
        own = slot_group == group
        far = slot_group != other_group
        reader = (slot_group - group) & 7
        owner = (other_group - group) & 7
        named = tuple(
            jnp.where(own & (slot_place == place), other, named[place])
            for place in range(PER_GROUP)
        )
        lowest = tuple(
            jnp.where(far & (owner == index), jnp.minimum(other_place, lowest[index]), lowest[index])
            for index in range(GROUPS)
        )
        highest = jnp.where(far & (owner == 0), jnp.maximum(other_place, highest), highest)
        chosen_place = tuple(
            jnp.where((owner == first) & (reader == second), other_place, current)
            for (first, second), current in zip(CHOICES, chosen_place)
        )
        wanted = tuple(
            jnp.where((owner == 0) & (reader == index), other_place, wanted[index])
            for index in range(GROUPS)
        )
        return named, lowest, highest, chosen_place, wanted

    zero = jnp.int32(0)
    named, lowest, highest, chosen_place, wanted = lax.fori_loop(
        0,
        PER_GROUP * GROUPS,
        read_links,
        (
            (zero,) * PER_GROUP,
            (zero + 7,) * GROUPS,
            zero,
            (zero,) * len(CHOICES),
            (zero - 1,) * GROUPS,
        ),
    )
    exports = (lowest[0], highest)
    chosen_second = tuple(
        place > lowest[owner] for (owner, _), place in zip(CHOICES, chosen_place)
    )
    offsets = tuple(((slot >> 3) - group) & 7 for slot in named)
    for place in range(PER_GROUP):
        index_k, index_v = zero, zero
        for offset in range(1, GROUPS):
            second = jnp.where((named[place] & 7) > lowest[offset], 1, 0)
            here = offsets[place] == offset
            start, views = POOL_K[offset]
            index_k = jnp.where(here, start + (second if views == 2 else 0), index_k)
            start, views = POOL_V[offset]
            index_v = jnp.where(here, start + (second if views == 2 else 0), index_v)
        before = zero - 1
        for earlier in range(place):
            before = jnp.where(
                (offsets[earlier] == offsets[place]) & (offsets[place] != 0), earlier, before
            )
        table[0, place] = index_k
        table[1, place] = index_v
        table[2, place] = jnp.where(offsets[place] == 0, 1, 0)
        table[3, place] = before

    def along_z(source, target, sends, receives, step):
        pltpu.make_async_remote_copy(
            src_ref=source,
            dst_ref=target,
            send_sem=sends,
            recv_sem=receives,
            device_id=((group + step) % GROUPS, head),
            device_id_type=MESH,
        ).start()

    pools = ((kh, stage_k, pool_k, z_recv_k, POOL_K), (vh, stage_v, pool_v, z_recv_v, POOL_V))

    def landing(array, offset):
        start, views = pools[array][4][offset]
        return pools[array][2].at[pl.ds(start, views)]

    def wait_landing(array, offset):
        here = landing(array, offset)
        pltpu.make_async_copy(here, here, pools[array][3].at[offset - 1]).wait()

    def first_hop(array):
        source, stage, _, receives, _ = pools[array]
        for index in range(2):
            stage[index] = source[pl.ds(exports[index] * RANKS, RANKS)]
        along_z(stage, landing(array, 7), z_send.at[array, 0], receives.at[6], 1)
        along_z(stage, landing(array, 1), z_send.at[array, 1], receives.at[0], 7)

    def forward(array, offset):
        step = 1 if offset > 3 else 7
        target = offset - 1 if step == 1 else offset + 1
        wait_landing(array, offset)
        along_z(
            landing(array, offset),
            landing(array, target),
            z_send.at[array, 1 + offset],
            pools[array][3].at[target - 1],
            step,
        )

    def forward_chosen(array, offset, index):
        step = 1 if offset > 3 else 7
        target = offset - 1 if step == 1 else offset + 1
        wait_landing(array, offset)
        start = pools[array][4][offset][0]
        pool = pools[array][2]
        chosen[index] = jnp.where(chosen_second[index], pool[start + 1], pool[start])
        along_z(
            chosen.at[pl.ds(index, 1)],
            landing(array, target),
            z_send.at[array, 1 + offset],
            pools[array][3].at[target - 1],
            step,
        )

    def heads_of(ref, place):
        return ref[pl.ds(place * RANKS, RANKS)].reshape(LENGTH, HD)

    def own_forward(place, carry):
        k, v, q = heads_of(kh, place), heads_of(vh, place), heads_of(qh, place)
        scores = dot_nt(k, q)
        top = EXP2_SCALE * jnp.max(scores, 0, keepdims=True)
        exps = jnp.exp2(scores * EXP2_SCALE - top)
        exp_own[place] = exps
        out_own[place] = dot_nn(v.T, exps.astype(BF))
        stats[place, 0:1] = top
        stats[place, 1:2] = jnp.sum(exps, 0, keepdims=True)
        return carry

    def far_part(place, carry):
        index_k, index_v = table[0, place], table[1, place]
        off = table[2, place].astype(F32) * 1e30
        before = table[3, place]
        rows = pl.ds(place * RANKS, RANKS)
        q, g = heads_of(qh, place), heads_of(gh, place)
        k, v = pool_k[index_k].reshape(LENGTH, HD), pool_v[index_v].reshape(LENGTH, HD)
        scores = dot_nt(k, q)
        own_top = stats[place, 0:1]
        top = jnp.maximum(own_top, EXP2_SCALE * jnp.max(scores, 0, keepdims=True) - off)
        exps = jnp.exp2(scores * EXP2_SCALE - (top + off))
        rescale = jnp.exp2(own_top - top)
        inverse = 1.0 / (stats[place, 1:2] * rescale + jnp.sum(exps, 0, keepdims=True))
        own_factor = rescale * inverse
        weights = exps * inverse
        weights_bf = weights.astype(BF)
        out = (out_own[place] * own_factor + dot_nn(v.T, weights_bf)).astype(BF)
        oh[rows] = out.T.reshape(RANKS, ROWS, HD)
        delta = jnp.sum(g.T.astype(F32) * out.astype(F32), 0, keepdims=True)
        dscore = (weights * (dot_nt(v, g) - delta)).astype(BF)
        d_far_all[place] = dscore
        stats[place, 2:3] = own_factor
        stats[place, 3:4] = delta
        chained = jnp.maximum(before, 0)
        old_k, old_v = acc_k[chained], acc_v[chained]
        acc_k[place] = dot_nn(dscore, q) * SCALE + jnp.where(before >= 0, old_k, 0.0)
        acc_v[place] = dot_nn(weights_bf, g) + jnp.where(before >= 0, old_v, 0.0)
        return carry

    def own_backward(place, carry):
        rows = pl.ds(place * RANKS, RANKS)
        k, v = heads_of(kh, place), heads_of(vh, place)
        q, g = heads_of(qh, place), heads_of(gh, place)
        far_k = pool_k[table[0, place]].reshape(LENGTH, HD)
        weights = exp_own[place] * stats[place, 2:3]
        dvh[rows] = dot_nn(weights.astype(BF), g).astype(BF).reshape(RANKS, ROWS, HD)
        dscore = (weights * (dot_nt(v, g) - stats[place, 3:4])).astype(BF)
        dkh[rows] = (dot_nn(dscore, q) * SCALE).astype(BF).reshape(RANKS, ROWS, HD)
        grad = (dot_nn(k.T, dscore) + dot_nn(far_k.T, d_far_all[place])) * SCALE
        dqh[rows] = grad.astype(BF).T.reshape(RANKS, ROWS, HD)
        return carry

    wait_heads(0, kh)
    first_hop(0)
    scatter_heads(2, q_in, qh)
    forward(0, 7)
    forward(0, 1)
    wait_heads(1, vh)
    first_hop(1)
    scatter_heads(3, g_in, gh)
    forward(0, 6)
    forward_chosen(0, 2, 1)
    forward(1, 7)
    forward(1, 1)
    forward_chosen(0, 5, 0)
    wait_heads(2, qh)
    lax.fori_loop(0, 2, own_forward, 0)
    forward_chosen(1, 6, 2)
    forward(1, 2)
    lax.fori_loop(2, 5, own_forward, 0)
    forward_chosen(1, 3, 3)
    lax.fori_loop(5, PER_GROUP, own_forward, 0)
    wait_heads(3, gh)
    wait_landing(0, 4)
    wait_landing(0, 3)
    wait_landing(1, 5)
    wait_landing(1, 4)
    lax.fori_loop(0, PER_GROUP, far_part, 0)

    returns = ((acc_k, ret_k, back_k, ret_recv_k), (acc_v, ret_v, back_v, ret_recv_v))
    order = (4, 3, 5, 2, 6, 1, 7)
    last = {}
    for offset in order:
        final = zero
        for place in range(PER_GROUP):
            final = jnp.where(offsets[place] == offset, place, final)
        last[offset] = final
    for rank in range(RANKS):
        for index, (acc, ret, back, recv) in enumerate(returns):
            for offset in order:
                ret[offset - 1, rank] = acc[last[offset], pl.ds(rank * ROWS, ROWS)].astype(BF)
                along_z(
                    ret.at[offset - 1, rank],
                    back.at[rank, OTHERS - offset],
                    ret_send.at[index],
                    recv.at[rank],
                    offset,
                )

    def gather_block(index, block, source, target):
        pltpu.make_async_remote_copy(
            src_ref=source.at[block],
            dst_ref=target.at[:, columns(head)],
            send_sem=out_send.at[index],
            recv_sem=out_recv.at[index],
            device_id=(group, block),
            device_id_type=MESH,
        ).start()

    def gather_own(index, source, target):
        pltpu.make_async_copy(
            source.at[head], target.at[:, columns(head)], out_recv.at[index]
        ).start()

    for_peers(lambda peer: gather_block(0, peer, oh, o_out))
    gather_own(0, oh, o_out)
    lax.fori_loop(0, PER_GROUP, own_backward, 0)
    for_peers(lambda peer: gather_block(1, peer, dqh, dq_out))
    gather_own(1, dqh, dq_out)

    for rank in range(RANKS):
        for index, (acc, ret, back, recv) in enumerate(returns):
            target = (dkh, dvh)[index]
            output = (dk_out, dv_out)[index]
            pltpu.make_async_copy(back.at[rank], back.at[rank], recv.at[rank]).wait()
            first_sum = jnp.zeros((ROWS, HD), F32)
            second_sum = jnp.zeros((ROWS, HD), F32)
            for offset in range(1, GROUPS):
                part = back[rank, offset - 1].astype(F32)
                first_sum += jnp.where(wanted[offset] == exports[0], part, 0.0)
                second_sum += jnp.where(wanted[offset] == exports[1], part, 0.0)
            for place in range(PER_GROUP):
                block = place * RANKS + rank
                extra = jnp.where(
                    place == exports[0],
                    first_sum,
                    jnp.where(place == exports[1], second_sum, 0.0),
                )
                target[block] = (target[block].astype(F32) + extra).astype(BF)

                @pl.when(block != head)
                def _():
                    gather_block(2 + index, block, target, output)

                @pl.when(block == head)
                def _():
                    gather_own(2 + index, target, output)

    for index, output in enumerate((o_out, dq_out, dk_out, dv_out)):
        pltpu.make_async_copy(output, output, out_recv.at[index]).wait()
    for index, source in enumerate((kh, vh, qh, gh)):
        blocks = source.at[pl.ds(0, HEADS - 1)]
        pltpu.make_async_copy(blocks, blocks, in_send.at[index]).wait()
        pltpu.make_async_copy(blocks, blocks, out_send.at[index]).wait()
    for array, stage in ((0, stage_k), (1, stage_v)):
        one = stage.at[pl.ds(0, 1)]
        pltpu.make_async_copy(stage, stage, z_send.at[array, 0]).wait()
        pltpu.make_async_copy(stage, stage, z_send.at[array, 1]).wait()
        for offset in ((7, 1, 6, 2, 5), (7, 1, 6, 2, 3))[array]:
            single = (array, offset) in ((0, 5), (0, 2), (1, 6), (1, 3))
            sent = one if single else stage
            pltpu.make_async_copy(sent, sent, z_send.at[array, 1 + offset]).wait()
    for index, ret in ((0, ret_k), (1, ret_v)):
        pltpu.make_async_copy(ret, ret, ret_send.at[index]).wait()


def on_device(query_tokens, key_tokens, value_tokens, cotangent, neighbors, view_slot):
    heads_buffer = pltpu.VMEM((HEADS, ROWS, HD), BF)

    def views(count):
        return pltpu.VMEM((count, RANKS, ROWS, HD), BF)

    back_buffer = pltpu.VMEM((RANKS, OTHERS, ROWS, HD), BF)
    sum_buffer = pltpu.VMEM((PER_GROUP, LENGTH, HD), F32)
    dma = pltpu.SemaphoreType.DMA
    smem = pl.BlockSpec(memory_space=pltpu.SMEM)
    anywhere = pl.BlockSpec(memory_space=pl.ANY)
    out = jax.ShapeDtypeStruct(query_tokens.shape, BF)
    return pl.pallas_call(
        kernel,
        out_shape=(out,) * 4,
        in_specs=[smem] * 2 + [anywhere] * 4,
        out_specs=(anywhere,) * 4,
        scratch_shapes=[heads_buffer] * 4
        + [views(2)] * 2
        + [views(len(CHOICES))]
        + [views(POOL)] * 2
        + [heads_buffer] * 4
        + [
            pltpu.VMEM((PER_GROUP, LENGTH, LENGTH), F32),
            pltpu.VMEM((PER_GROUP, HD, LENGTH), F32),
            pltpu.VMEM((PER_GROUP, 8, LENGTH), F32),
            pltpu.VMEM((PER_GROUP, LENGTH, LENGTH), BF),
        ]
        + [sum_buffer] * 2
        + [views(OTHERS)] * 2
        + [back_buffer] * 2
        + [pltpu.SMEM((4, PER_GROUP), jnp.int32)]
        + [dma((4,))] * 2
        + [dma((2, 9))]
        + [dma((OTHERS,))] * 2
        + [dma((2,))]
        + [dma((RANKS,))] * 2
        + [dma((4,))] * 2,
        compiler_params=pltpu.CompilerParams(
            collective_id=0, has_side_effects=True, vmem_limit_bytes=56 << 20
        ),
    )(neighbors.T, view_slot, query_tokens, key_tokens, value_tokens, cotangent)


def solution(mesh):
    rows = P(("view", "head"), None)
    return jax.shard_map(
        on_device,
        mesh=mesh,
        in_specs=(rows, rows, rows, rows, P(), P()),
        out_specs=(rows, rows, rows, rows),
        check_vma=False,
    )
```

time: 161 us -> 143 us (0.89)
  Pallas kernels: 153 us -> 135 us
    pallas_call x1, Pallas kernels: 153 us -> 135 us  [on_device(): pl.pallas_call(kernel, out_shape=(out,) * 4, in_specs=[smem] * 2 + [anywh...]
    unnamed x11 -> x10, local copies, waits for them, and re-layouts: 7.94 us -> 6.55 us
where the time goes in v2:
time: 143 us; the launch traced here: 142 us
  Pallas kernels  135 us (94%)
  local copies, waits for them, and re-layouts  6.55 us (5%)
    pallas_call x1, Pallas kernels, on_device(): pl.pallas_call(kernel, out_shape=(out,) * 4, in_specs=[smem] * 2 + [anywh...  135 us
    unnamed x10, local copies, waits for them, and re-layouts  6.55 us

profile of v2, /device:TPU:3, one launch (start us, length us, event | category | flops | bytes accessed | tf_op | source)
XLA Modules:
  0.0 142.1 jit_solution(9452929782200275450)
XLA Ops:
  0.6 134.9 %shard_map.93 = (bf16[128,4096]{1,0:T(8,128)(2,1)}, bf16[128,4096]{1,0:T(8,128)(2,1)}, bf16[128,4096]{1,0:T(8,128)(2,1)}, bf16[128,4096]{1,0:T(8,128)(2,1)}) custom-call(s32[2,64]{1,0:T(2,128)} %bitcast.1, s32[64]{0:T(128)} %view_slot.1, bf16[128,4096]{1,0:T(8,128)(2,1)} %q_in.1, bf16[128,4096]{1,0:T(8,128)(2,1)} %k_in.1, bf16[128,4096]{1,0:T(8,128)(2,1)} %v_in.1, ...), custom_call_target="tpu_custom_call" | custom-call | tf_op jit(solution)/shard_map/pallas_call | solution.py:414
  135.5 0.0 copy-start.2
  135.5 2.4 %copy.14 = bf16[128,4096]{1,0:T(8,128)(2,1)} copy(bf16[128,4096]{1,0:T(8,128)(2,1)} %get-tuple-element.8) | data formatting | bytes 2097152
  137.9 0.0 copy-done.2
  137.9 0.0 copy-start.1
  137.9 1.0 copy.15
  138.9 0.6 copy-done.1
  139.5 0.0 copy-start
  139.5 1.0 copy.16
  140.5 0.6 copy-done
  141.1 1.0 copy.17
Async XLA Ops:
  135.5 2.4 %copy-start.2 = (bf16[128,4096]{1,0:T(8,128)(2,1)S(1)}, bf16[128,4096]{1,0:T(8,128)(2,1)}, u32[]{:S(2)}) copy-start(bf16[128,4096]{1,0:T(8,128)(2,1)} %get-tuple-element.9) | copy-start | bytes 3145732
  137.9 1.6 %copy-start.1 = (bf16[128,4096]{1,0:T(8,128)(2,1)S(1)}, bf16[128,4096]{1,0:T(8,128)(2,1)}, u32[]{:S(2)}) copy-start(bf16[128,4096]{1,0:T(8,128)(2,1)} %get-tuple-element.10) | copy-start | bytes 3145732
  139.5 1.6 %copy-start = (bf16[128,4096]{1,0:T(8,128)(2,1)S(1)}, bf16[128,4096]{1,0:T(8,128)(2,1)}, u32[]{:S(2)}) copy-start(bf16[128,4096]{1,0:T(8,128)(2,1)} %get-tuple-element.11) | copy-start | bytes 3145732

commit v3 on v2

--- a/solution.py
+++ b/solution.py
@@ -17,6 +17,7 @@
 HD = 128
 LENGTH = 512
 OTHERS = GROUPS - 1
+PARTS = 4
 SCALE = 1.0 / math.sqrt(HD)
 EXP2_SCALE = math.log2(math.e) / math.sqrt(HD)
 BF = jnp.bfloat16
@@ -58,7 +59,7 @@
     qh, kh, vh, gh,
     stage_k, stage_v, chosen, pool_k, pool_v,
     oh, dqh, dkh, dvh,
-    exp_own, out_own, stats, d_far_all,
+    exp_own, out_own, stats, weights_far, d_far_all,
     acc_k, acc_v, ret_k, ret_v, back_k, back_v,
     table,
     in_send, in_recv, z_send, z_recv_k, z_recv_v,
@@ -187,47 +188,58 @@
 
     pools = ((kh, stage_k, pool_k, z_recv_k, POOL_K), (vh, stage_v, pool_v, z_recv_v, POOL_V))
 
-    def landing(array, offset):
+    def landing(array, offset, rank):
         start, views = pools[array][4][offset]
-        return pools[array][2].at[pl.ds(start, views)]
-
-    def wait_landing(array, offset):
-        here = landing(array, offset)
-        pltpu.make_async_copy(here, here, pools[array][3].at[offset - 1]).wait()
+        return pools[array][2].at[pl.ds(start, views), rank]
+
+    def landed(array, offset, rank):
+        return pools[array][3].at[offset - 1, rank]
+
+    def wait_landing(array, offset, rank):
+        here = landing(array, offset, rank)
+        pltpu.make_async_copy(here, here, landed(array, offset, rank)).wait()
 
     def first_hop(array):
-        source, stage, _, receives, _ = pools[array]
-        for index in range(2):
-            stage[index] = source[pl.ds(exports[index] * RANKS, RANKS)]
-        along_z(stage, landing(array, 7), z_send.at[array, 0], receives.at[6], 1)
-        along_z(stage, landing(array, 1), z_send.at[array, 1], receives.at[0], 7)
-
-    def forward(array, offset):
+        source, stage = pools[array][:2]
+        for rank in range(RANKS):
+            for index in range(2):
+                stage[index, rank] = source[exports[index] * RANKS + rank]
+            for offset, step, sends in ((7, 1, 0), (1, 7, 8)):
+                along_z(
+                    stage.at[:, rank],
+                    landing(array, offset, rank),
+                    z_send.at[array, sends],
+                    landed(array, offset, rank),
+                    step,
+                )
+
+    def forward(array, offset, rank, choice=None):
         step = 1 if offset > 3 else 7
         target = offset - 1 if step == 1 else offset + 1
-        wait_landing(array, offset)
+        wait_landing(array, offset, rank)
+        source = landing(array, offset, rank)
+        if choice is not None:
+            start, pool = pools[array][4][offset][0], pools[array][2]
+            chosen[choice, rank] = jnp.where(
+                chosen_second[choice], pool[start + 1, rank], pool[start, rank]
+            )
+            source = chosen.at[pl.ds(choice, 1), rank]
         along_z(
-            landing(array, offset),
-            landing(array, target),
-            z_send.at[array, 1 + offset],
-            pools[array][3].at[target - 1],
+            source,
+            landing(array, target, rank),
+            z_send.at[array, offset],
+            landed(array, target, rank),
             step,
         )
 
-    def forward_chosen(array, offset, index):
-        step = 1 if offset > 3 else 7
-        target = offset - 1 if step == 1 else offset + 1
-        wait_landing(array, offset)
-        start = pools[array][4][offset][0]
-        pool = pools[array][2]
-        chosen[index] = jnp.where(chosen_second[index], pool[start + 1], pool[start])
-        along_z(
-            chosen.at[pl.ds(index, 1)],
-            landing(array, target),
-            z_send.at[array, 1 + offset],
-            pools[array][3].at[target - 1],
-            step,
-        )
+    hops = (
+        (((7, None), (1, None)), ((6, None), (2, 1)), ((5, 0),)),
+        (((7, None), (1, None)), ((6, 2), (2, None)), ((3, 3),)),
+    )
+
+    def hop(array, stage, rank):
+        for offset, choice in hops[array][stage]:
+            forward(array, offset, rank, choice)
 
     def heads_of(ref, place):
         return ref[pl.ds(place * RANKS, RANKS)].reshape(LENGTH, HD)
@@ -243,13 +255,17 @@
         stats[place, 1:2] = jnp.sum(exps, 0, keepdims=True)
         return carry
 
-    def far_part(place, carry):
-        index_k, index_v = table[0, place], table[1, place]
+    def chain(acc, place, part):
+        before = table[3, place]
+        old = acc[jnp.maximum(before, 0)]
+        acc[place] = part + jnp.where(before >= 0, old, 0.0)
+
+    def far_weights(place, carry):
         off = table[2, place].astype(F32) * 1e30
-        before = table[3, place]
         rows = pl.ds(place * RANKS, RANKS)
         q, g = heads_of(qh, place), heads_of(gh, place)
-        k, v = pool_k[index_k].reshape(LENGTH, HD), pool_v[index_v].reshape(LENGTH, HD)
+        k = pool_k[table[0, place]].reshape(LENGTH, HD)
+        v = pool_v[table[1, place]].reshape(LENGTH, HD)
         scores = dot_nt(k, q)
         own_top = stats[place, 0:1]
         top = jnp.maximum(own_top, EXP2_SCALE * jnp.max(scores, 0, keepdims=True) - off)
@@ -258,18 +274,21 @@
         inverse = 1.0 / (stats[place, 1:2] * rescale + jnp.sum(exps, 0, keepdims=True))
         own_factor = rescale * inverse
         weights = exps * inverse
+        weights_far[place] = weights
         weights_bf = weights.astype(BF)
         out = (out_own[place] * own_factor + dot_nn(v.T, weights_bf)).astype(BF)
         oh[rows] = out.T.reshape(RANKS, ROWS, HD)
-        delta = jnp.sum(g.T.astype(F32) * out.astype(F32), 0, keepdims=True)
-        dscore = (weights * (dot_nt(v, g) - delta)).astype(BF)
+        stats[place, 2:3] = own_factor
+        stats[place, 3:4] = jnp.sum(g.T.astype(F32) * out.astype(F32), 0, keepdims=True)
+        chain(acc_v, place, dot_nn(weights_bf, g))
+        return carry
+
+    def far_scores(place, carry):
+        q, g = heads_of(qh, place), heads_of(gh, place)
+        v = pool_v[table[1, place]].reshape(LENGTH, HD)
+        dscore = (weights_far[place] * (dot_nt(v, g) - stats[place, 3:4])).astype(BF)
         d_far_all[place] = dscore
-        stats[place, 2:3] = own_factor
-        stats[place, 3:4] = delta
-        chained = jnp.maximum(before, 0)
-        old_k, old_v = acc_k[chained], acc_v[chained]
-        acc_k[place] = dot_nn(dscore, q) * SCALE + jnp.where(before >= 0, old_k, 0.0)
-        acc_v[place] = dot_nn(weights_bf, g) + jnp.where(before >= 0, old_v, 0.0)
+        chain(acc_k, place, dot_nn(dscore, q) * SCALE)
         return carry
 
     def own_backward(place, carry):
@@ -288,29 +307,26 @@
     wait_heads(0, kh)
     first_hop(0)
     scatter_heads(2, q_in, qh)
-    forward(0, 7)
-    forward(0, 1)
+    for stage in range(2):
+        for rank in range(RANKS):
+            hop(0, stage, rank)
     wait_heads(1, vh)
     first_hop(1)
     scatter_heads(3, g_in, gh)
-    forward(0, 6)
-    forward_chosen(0, 2, 1)
-    forward(1, 7)
-    forward(1, 1)
-    forward_chosen(0, 5, 0)
+    for rank in range(RANKS):
+        hop(0, 2, rank)
+    for rank in range(RANKS):
+        hop(1, 0, rank)
     wait_heads(2, qh)
-    lax.fori_loop(0, 2, own_forward, 0)
-    forward_chosen(1, 6, 2)
-    forward(1, 2)
-    lax.fori_loop(2, 5, own_forward, 0)
-    forward_chosen(1, 3, 3)
-    lax.fori_loop(5, PER_GROUP, own_forward, 0)
+    for stage in range(1, 3):
+        for rank in range(RANKS):
+            hop(1, stage, rank)
+            lax.fori_loop(4 * stage + rank - 4, 4 * stage + rank - 3, own_forward, 0)
     wait_heads(3, gh)
-    wait_landing(0, 4)
-    wait_landing(0, 3)
-    wait_landing(1, 5)
-    wait_landing(1, 4)
-    lax.fori_loop(0, PER_GROUP, far_part, 0)
+    for rank in range(RANKS):
+        for array, offset in ((0, 4), (0, 3), (1, 5), (1, 4)):
+            wait_landing(array, offset, rank)
+    lax.fori_loop(0, PER_GROUP, far_weights, 0)
 
     returns = ((acc_k, ret_k, back_k, ret_recv_k), (acc_v, ret_v, back_v, ret_recv_v))
     order = (4, 3, 5, 2, 6, 1, 7)
@@ -320,8 +336,10 @@
         for place in range(PER_GROUP):
             final = jnp.where(offsets[place] == offset, place, final)
         last[offset] = final
-    for rank in range(RANKS):
-        for index, (acc, ret, back, recv) in enumerate(returns):
+
+    def send_returns(index):
+        acc, ret, back, recv = returns[index]
+        for rank in range(RANKS):
             for offset in order:
                 ret[offset - 1, rank] = acc[last[offset], pl.ds(rank * ROWS, ROWS)].astype(BF)
                 along_z(
@@ -347,14 +365,18 @@
             source.at[head], target.at[:, columns(head)], out_recv.at[index]
         ).start()
 
+    send_returns(1)
     for_peers(lambda peer: gather_block(0, peer, oh, o_out))
     gather_own(0, oh, o_out)
+    lax.fori_loop(0, PER_GROUP, far_scores, 0)
+    send_returns(0)
     lax.fori_loop(0, PER_GROUP, own_backward, 0)
     for_peers(lambda peer: gather_block(1, peer, dqh, dq_out))
     gather_own(1, dqh, dq_out)
 
-    for rank in range(RANKS):
-        for index, (acc, ret, back, recv) in enumerate(returns):
+    for index in (1, 0):
+        for rank in range(RANKS):
+            acc, ret, back, recv = returns[index]
             target = (dkh, dvh)[index]
             output = (dk_out, dv_out)[index]
             pltpu.make_async_copy(back.at[rank], back.at[rank], recv.at[rank]).wait()
@@ -389,14 +411,19 @@
         pltpu.make_async_copy(blocks, blocks, out_send.at[index]).wait()
     for array, stage in ((0, stage_k), (1, stage_v)):
         one = stage.at[pl.ds(0, 1)]
-        pltpu.make_async_copy(stage, stage, z_send.at[array, 0]).wait()
-        pltpu.make_async_copy(stage, stage, z_send.at[array, 1]).wait()
-        for offset in ((7, 1, 6, 2, 5), (7, 1, 6, 2, 3))[array]:
-            single = (array, offset) in ((0, 5), (0, 2), (1, 6), (1, 3))
-            sent = one if single else stage
-            pltpu.make_async_copy(sent, sent, z_send.at[array, 1 + offset]).wait()
+        for sends in (0, 8):
+            pltpu.make_async_copy(stage, stage, z_send.at[array, sends]).wait()
+        for level in hops[array]:
+            for offset, choice in level:
+                sent = stage if choice is None else one
+                pltpu.make_async_copy(sent, sent, z_send.at[array, offset]).wait()
     for index, ret in ((0, ret_k), (1, ret_v)):
         pltpu.make_async_copy(ret, ret, ret_send.at[index]).wait()
+
+
+def hand_over(*refs):
+    for index in range(4):
+        refs[4 + index][...] = refs[index][...]
 
 
 def on_device(query_tokens, key_tokens, value_tokens, cotangent, neighbors, view_slot):
@@ -411,7 +438,7 @@
     smem = pl.BlockSpec(memory_space=pltpu.SMEM)
     anywhere = pl.BlockSpec(memory_space=pl.ANY)
     out = jax.ShapeDtypeStruct(query_tokens.shape, BF)
-    return pl.pallas_call(
+    results = pl.pallas_call(
         kernel,
         out_shape=(out,) * 4,
         in_specs=[smem] * 2 + [anywhere] * 4,
@@ -425,6 +452,7 @@
             pltpu.VMEM((PER_GROUP, LENGTH, LENGTH), F32),
             pltpu.VMEM((PER_GROUP, HD, LENGTH), F32),
             pltpu.VMEM((PER_GROUP, 8, LENGTH), F32),
+            pltpu.VMEM((PER_GROUP, LENGTH, LENGTH), F32),
             pltpu.VMEM((PER_GROUP, LENGTH, LENGTH), BF),
         ]
         + [sum_buffer] * 2
@@ -433,7 +461,7 @@
         + [pltpu.SMEM((4, PER_GROUP), jnp.int32)]
         + [dma((4,))] * 2
         + [dma((2, 9))]
-        + [dma((OTHERS,))] * 2
+        + [dma((OTHERS, RANKS))] * 2
         + [dma((2,))]
         + [dma((RANKS,))] * 2
         + [dma((4,))] * 2,
@@ -441,6 +469,14 @@
             collective_id=0, has_side_effects=True, vmem_limit_bytes=56 << 20
         ),
     )(neighbors.T, view_slot, query_tokens, key_tokens, value_tokens, cotangent)
+    block = pl.BlockSpec((ROWS // PARTS, query_tokens.shape[1]), lambda part: (part, 0))
+    return pl.pallas_call(
+        hand_over,
+        grid=(PARTS,),
+        out_shape=(out,) * 4,
+        in_specs=[block] * 4,
+        out_specs=(block,) * 4,
+    )(*results)
 
 
 def solution(mesh):

time: 143 us -> 136 us (0.951)
  local copies, waits for them, and re-layouts: 6.55 us -> 0 us
    unnamed x10 -> x0, local copies, waits for them, and re-layouts: 6.55 us -> none
    pallas_call x0 -> x1, Pallas kernels: none -> 4.66 us  [on_device(): pl.pallas_call(hand_over, grid=(PARTS,), out_shape=(out,) * 4, in_specs=[...]
    pallas_call x1, Pallas kernels: 135 us -> 131 us  [on_device(): pl.pallas_call(kernel, out_shape=(out,) * 4, in_specs=[smem] * 2 + [anywh...]
where the time goes in v3:
time: 136 us
  Pallas kernels  135 us (99%)
    pallas_call x1, Pallas kernels, on_device(): pl.pallas_call(kernel, out_shape=(out,) * 4, in_specs=[smem] * 2 + [anywh...  131 us
    pallas_call x1, Pallas kernels, on_device(): pl.pallas_call(hand_over, grid=(PARTS,), out_shape=(out,) * 4, in_specs=[...  4.66 us

profile of v3, /device:TPU:3, one launch (start us, length us, event | category | flops | bytes accessed | tf_op | source)
XLA Modules:
  0.0 135.9 jit_solution(14378687290594438517)
XLA Ops:
  0.6 130.6 %shard_map.93 = (bf16[128,4096]{1,0:T(8,128)(2,1)}, bf16[128,4096]{1,0:T(8,128)(2,1)}, bf16[128,4096]{1,0:T(8,128)(2,1)}, bf16[128,4096]{1,0:T(8,128)(2,1)}) custom-call(s32[2,64]{1,0:T(2,128)} %bitcast.1, s32[64]{0:T(128)} %view_slot.1, bf16[128,4096]{1,0:T(8,128)(2,1)} %q_in.1, bf16[128,4096]{1,0:T(8,128)(2,1)} %k_in.1, bf16[128,4096]{1,0:T(8,128)(2,1)} %v_in.1, ...), custom_call_target="tpu_custom_call" | custom-call | tf_op jit(solution)/shard_map/pallas_call | solution.py:441
  131.2 4.7 %shard_map.94 = (bf16[128,4096]{1,0:T(8,128)(2,1)}, bf16[128,4096]{1,0:T(8,128)(2,1)}, bf16[128,4096]{1,0:T(8,128)(2,1)}, bf16[128,4096]{1,0:T(8,128)(2,1)}) custom-call(bf16[128,4096]{1,0:T(8,128)(2,1)} %get-tuple-element.8.refs_0_, bf16[128,4096]{1,0:T(8,128)(2,1)} %get-tuple-element.9.refs_1_, bf16[128,4096]{1,0:T(8,128)(2,1)} %get-tuple-element.10.refs_2_, ...), custom_call_target="tpu_custom_call" | custom-call | tf_op jit(solution)/shard_map/pallas_call | solution.py:473

commit v4 on v3

--- a/solution.py
+++ b/solution.py
@@ -262,23 +262,24 @@
 
     def far_weights(place, carry):
         off = table[2, place].astype(F32) * 1e30
-        rows = pl.ds(place * RANKS, RANKS)
-        q, g = heads_of(qh, place), heads_of(gh, place)
-        k = pool_k[table[0, place]].reshape(LENGTH, HD)
-        v = pool_v[table[1, place]].reshape(LENGTH, HD)
-        scores = dot_nt(k, q)
+        scores = dot_nt(pool_k[table[0, place]].reshape(LENGTH, HD), heads_of(qh, place))
         own_top = stats[place, 0:1]
         top = jnp.maximum(own_top, EXP2_SCALE * jnp.max(scores, 0, keepdims=True) - off)
         exps = jnp.exp2(scores * EXP2_SCALE - (top + off))
         rescale = jnp.exp2(own_top - top)
         inverse = 1.0 / (stats[place, 1:2] * rescale + jnp.sum(exps, 0, keepdims=True))
         own_factor = rescale * inverse
-        weights = exps * inverse
-        weights_far[place] = weights
-        weights_bf = weights.astype(BF)
-        out = (out_own[place] * own_factor + dot_nn(v.T, weights_bf)).astype(BF)
+        weights_far[place] = exps * inverse
+        stats[place, 2:3] = own_factor
+        return carry
+
+    def far_values(place, carry):
+        rows = pl.ds(place * RANKS, RANKS)
+        g = heads_of(gh, place)
+        v = pool_v[table[1, place]].reshape(LENGTH, HD)
+        weights_bf = weights_far[place].astype(BF)
+        out = (out_own[place] * stats[place, 2:3] + dot_nn(v.T, weights_bf)).astype(BF)
         oh[rows] = out.T.reshape(RANKS, ROWS, HD)
-        stats[place, 2:3] = own_factor
         stats[place, 3:4] = jnp.sum(g.T.astype(F32) * out.astype(F32), 0, keepdims=True)
         chain(acc_v, place, dot_nn(weights_bf, g))
         return carry
@@ -318,15 +319,20 @@
     for rank in range(RANKS):
         hop(1, 0, rank)
     wait_heads(2, qh)
-    for stage in range(1, 3):
-        for rank in range(RANKS):
-            hop(1, stage, rank)
-            lax.fori_loop(4 * stage + rank - 4, 4 * stage + rank - 3, own_forward, 0)
+    for rank in range(RANKS):
+        hop(1, 1, rank)
+        lax.fori_loop(2 * rank, 2 * rank + 2, own_forward, 0, unroll=2)
+    for rank in range(RANKS):
+        wait_landing(0, 4, rank)
+        wait_landing(0, 3, rank)
+    for rank in range(RANKS):
+        hop(1, 2, rank)
+        lax.fori_loop(2 * rank, 2 * rank + 2, far_weights, 0, unroll=2)
     wait_heads(3, gh)
     for rank in range(RANKS):
-        for array, offset in ((0, 4), (0, 3), (1, 5), (1, 4)):
-            wait_landing(array, offset, rank)
-    lax.fori_loop(0, PER_GROUP, far_weights, 0)
+        wait_landing(1, 5, rank)
+        wait_landing(1, 4, rank)
+    lax.fori_loop(0, PER_GROUP, far_values, 0, unroll=2)
 
     returns = ((acc_k, ret_k, back_k, ret_recv_k), (acc_v, ret_v, back_v, ret_recv_v))
     order = (4, 3, 5, 2, 6, 1, 7)
@@ -368,9 +374,9 @@
     send_returns(1)
     for_peers(lambda peer: gather_block(0, peer, oh, o_out))
     gather_own(0, oh, o_out)
-    lax.fori_loop(0, PER_GROUP, far_scores, 0)
+    lax.fori_loop(0, PER_GROUP, far_scores, 0, unroll=2)
     send_returns(0)
-    lax.fori_loop(0, PER_GROUP, own_backward, 0)
+    lax.fori_loop(0, PER_GROUP, own_backward, 0, unroll=2)
     for_peers(lambda peer: gather_block(1, peer, dqh, dq_out))
     gather_own(1, dqh, dq_out)
 

time: 136 us -> 129 us (0.949)
  Pallas kernels: 135 us -> 129 us
    pallas_call x1, Pallas kernels: 131 us -> 124 us  [on_device(): pl.pallas_call(kernel, out_shape=(out,) * 4, in_specs=[smem] * 2 + [anywh...]
where the time goes in v4:
time: 129 us
  Pallas kernels  129 us (100%)
    pallas_call x1, Pallas kernels, on_device(): pl.pallas_call(kernel, out_shape=(out,) * 4, in_specs=[smem] * 2 + [anywh...  124 us
    pallas_call x1, Pallas kernels, on_device(): pl.pallas_call(hand_over, grid=(PARTS,), out_shape=(out,) * 4, in_specs=[...  4.66 us

profile of v4, /device:TPU:3, one launch (start us, length us, event | category | flops | bytes accessed | tf_op | source)
XLA Modules:
  0.0 129.2 jit_solution(2255367040877340377)
XLA Ops:
  0.6 123.9 %shard_map.93 = (bf16[128,4096]{1,0:T(8,128)(2,1)}, bf16[128,4096]{1,0:T(8,128)(2,1)}, bf16[128,4096]{1,0:T(8,128)(2,1)}, bf16[128,4096]{1,0:T(8,128)(2,1)}) custom-call(s32[2,64]{1,0:T(2,128)} %bitcast.1, s32[64]{0:T(128)} %view_slot.1, bf16[128,4096]{1,0:T(8,128)(2,1)} %q_in.1, bf16[128,4096]{1,0:T(8,128)(2,1)} %k_in.1, bf16[128,4096]{1,0:T(8,128)(2,1)} %v_in.1, ...), custom_call_target="tpu_custom_call" | custom-call | tf_op jit(solution)/shard_map/pallas_call | solution.py:447
  124.6 4.7 %shard_map.94 = (bf16[128,4096]{1,0:T(8,128)(2,1)}, bf16[128,4096]{1,0:T(8,128)(2,1)}, bf16[128,4096]{1,0:T(8,128)(2,1)}, bf16[128,4096]{1,0:T(8,128)(2,1)}) custom-call(bf16[128,4096]{1,0:T(8,128)(2,1)} %get-tuple-element.8.refs_0_, bf16[128,4096]{1,0:T(8,128)(2,1)} %get-tuple-element.9.refs_1_, bf16[128,4096]{1,0:T(8,128)(2,1)} %get-tuple-element.10.refs_2_, ...), custom_call_target="tpu_custom_call" | custom-call | tf_op jit(solution)/shard_map/pallas_call | solution.py:479

commit v5 on v4

--- a/solution.py
+++ b/solution.py
@@ -332,7 +332,7 @@
     for rank in range(RANKS):
         wait_landing(1, 5, rank)
         wait_landing(1, 4, rank)
-    lax.fori_loop(0, PER_GROUP, far_values, 0, unroll=2)
+    lax.fori_loop(0, PER_GROUP, far_values, 0, unroll=4)
 
     returns = ((acc_k, ret_k, back_k, ret_recv_k), (acc_v, ret_v, back_v, ret_recv_v))
     order = (4, 3, 5, 2, 6, 1, 7)
@@ -376,9 +376,23 @@
     gather_own(0, oh, o_out)
     lax.fori_loop(0, PER_GROUP, far_scores, 0, unroll=2)
     send_returns(0)
-    lax.fori_loop(0, PER_GROUP, own_backward, 0, unroll=2)
-    for_peers(lambda peer: gather_block(1, peer, dqh, dq_out))
-    gather_own(1, dqh, dq_out)
+    def own_backward_pair(pair, carry):
+        for view in range(2):
+            own_backward(2 * pair + view, carry)
+        for index in range(2 * RANKS):
+            block = 2 * RANKS * pair + index
+
+            @pl.when(block != head)
+            def _():
+                gather_block(1, block, dqh, dq_out)
+
+            @pl.when(block == head)
+            def _():
+                gather_own(1, dqh, dq_out)
+
+        return carry
+
+    lax.fori_loop(0, PER_GROUP // 2, own_backward_pair, 0)
 
     for index in (1, 0):
         for rank in range(RANKS):

time: 129 us -> 129 us (level)
  no operation moved by 1% of the time
where the time goes in v5:
time: 129 us
  Pallas kernels  128 us (99%)
    pallas_call x1, Pallas kernels, on_device(): pl.pallas_call(kernel, out_shape=(out,) * 4, in_specs=[smem] * 2 + [anywh...  123 us
    pallas_call x1, Pallas kernels, on_device(): pl.pallas_call(hand_over, grid=(PARTS,), out_shape=(out,) * 4, in_specs=[...  4.66 us

profile of v5, /device:TPU:3, one launch (start us, length us, event | category | flops | bytes accessed | tf_op | source)
XLA Modules:
  0.0 128.6 jit_solution(6545567519891001766)
XLA Ops:
  0.6 123.3 %shard_map.93 = (bf16[128,4096]{1,0:T(8,128)(2,1)}, bf16[128,4096]{1,0:T(8,128)(2,1)}, bf16[128,4096]{1,0:T(8,128)(2,1)}, bf16[128,4096]{1,0:T(8,128)(2,1)}) custom-call(s32[2,64]{1,0:T(2,128)} %bitcast.1, s32[64]{0:T(128)} %view_slot.1, bf16[128,4096]{1,0:T(8,128)(2,1)} %q_in.1, bf16[128,4096]{1,0:T(8,128)(2,1)} %k_in.1, bf16[128,4096]{1,0:T(8,128)(2,1)} %v_in.1, ...), custom_call_target="tpu_custom_call" | custom-call | tf_op jit(solution)/shard_map/pallas_call | solution.py:461
  123.9 4.7 %shard_map.94 = (bf16[128,4096]{1,0:T(8,128)(2,1)}, bf16[128,4096]{1,0:T(8,128)(2,1)}, bf16[128,4096]{1,0:T(8,128)(2,1)}, bf16[128,4096]{1,0:T(8,128)(2,1)}) custom-call(bf16[128,4096]{1,0:T(8,128)(2,1)} %get-tuple-element.8.refs_0_, bf16[128,4096]{1,0:T(8,128)(2,1)} %get-tuple-element.9.refs_1_, bf16[128,4096]{1,0:T(8,128)(2,1)} %get-tuple-element.10.refs_2_, ...), custom_call_target="tpu_custom_call" | custom-call | tf_op jit(solution)/shard_map/pallas_call | solution.py:493
